TPU v7x, 256 devices: a whole 4x4x8 slice. The times are simulated.
256 devices in a mesh: ex: 32 (over y, z), lay: 8 (over x, core).
Axes of the slice: x: 4, y: 4, z: 8, core: 2. Of those that a mesh axis runs over, the one named last changes fastest.
Arguments:
- acts: bfloat16 [65536, 5120], P('ex', 'lay'), may hold values from -6 to 6
- grads: bfloat16 [65536, 13824], P('ex', 'lay'), may hold values from -6 to 6
- act_basis: bfloat16 [5120, 5120], P('lay', 'ex'), may hold values from -0.078125 to 0.078125
- grad_basis: bfloat16 [13824, 13824], P('lay', 'ex'), may hold values from -0.0546875 to 0.0546875
- act_query: bfloat16 [5120, 512], P('ex'), may hold values from -0.078125 to 0.078125
- grad_query: bfloat16 [13824, 512], P('ex'), may hold values from -0.0546875 to 0.0546875
- lengths: int32 [64], P('ex'), may hold values from 1 to 1024, as said below
- destination: int32 [64], P('ex'), may hold values from 0 to 63, each once
Outputs:
- scores: float32 [64, 16], P('ex', 'lay')
Inputs may be any that keep to these rules, and one draw needn't show every extreme that they name: The lengths of one index of ex are its 2 packed examples in order; their sum is at most 2048, and in every draw some index of ex is exactly full. `destination`: each output row is named by exactly one packed example.
All inputs are finite; a program needn't handle non-finite values.
Results may differ from a plain program's by a relative error of at most 0.0042.
Values may be sent and summed in bfloat16 or wider, within the bound.
A program may use at most 128 MiB of HBM per device.

v0:
```python
import math

import jax
import jax.numpy as jnp
from jax import lax
from jax.sharding import PartitionSpec as P

RANK = 32
LMAX = 1024


def shards(acts, grads, act_basis, grad_basis, act_query, grad_query, lengths, destination):
    grad_part = jnp.dot(grad_basis, grad_query, preferred_element_type=jnp.float32)
    act_part = jnp.dot(act_basis, act_query, preferred_element_type=jnp.float32)
    grad_sum, act_sum = lax.psum((grad_part, act_part), "ex")
    grad_rot = grad_sum.astype(jnp.bfloat16)
    act_rot = act_sum.astype(jnp.bfloat16)
    tok_count = acts.shape[0]
    columns = grad_query.shape[1]
    share = columns // lax.axis_size("lay")
    grad_part = jnp.einsum("tf,fc->ct", grads, grad_rot, preferred_element_type=jnp.float32)
    act_part = jnp.einsum("tf,fc->ct", acts, act_rot, preferred_element_type=jnp.float32)
    projected = lax.psum_scatter(
        jnp.stack([grad_part, act_part], axis=1), "lay", scatter_dimension=0, tiled=True
    )
    query_count = share // RANK
    paired = projected.reshape(query_count, RANK, 2, tok_count)
    token_score = jnp.sum(paired[:, :, 0, :] * paired[:, :, 1, :], axis=1)
    ends = jnp.cumsum(lengths)
    starts = ends - lengths
    offsets = jnp.arange(tok_count, dtype=jnp.int32)
    member = ((offsets[None, :] >= starts[:, None]) & (offsets[None, :] < ends[:, None])).astype(
        jnp.float32
    )
    factor = 1.0 / math.sqrt(LMAX * RANK)
    packed = (
        lax.dot_general(
            member, token_score, (((1,), (1,)), ((), ())), precision=lax.Precision.HIGHEST
        )
        * factor
    )
    ex_count = lengths.shape[0]
    every_score, every_target = (
        lax.all_gather(packed, "ex", axis=0, tiled=True),
        lax.all_gather(destination, "ex", axis=0, tiled=True),
    )
    owned = lax.axis_index("ex") * ex_count + jnp.arange(ex_count, dtype=jnp.int32)
    picker = (every_target[None, :] == owned[:, None]).astype(jnp.float32)
    scores = jnp.dot(picker, every_score, precision=lax.Precision.HIGHEST)
    return scores


def solution(mesh):
    return jax.shard_map(
        shards,
        mesh=mesh,
        in_specs=(
            P("ex", "lay"),
            P("ex", "lay"),
            P("lay", "ex"),
            P("lay", "ex"),
            P("ex", None),
            P("ex", None),
            P("ex"),
            P("ex"),
        ),
        out_specs=P("ex", "lay"),
        check_vma=False,
    )
```

profile of v0, /device:TPU:8, one launch (start us, length us, event | category | flops | bytes accessed | tf_op | source)
XLA Modules:
  0.0 306.7 jit_solution(14337094986568716186)
XLA Ops:
  6.5 0.0 copy-start
  6.5 0.0 copy-start.1
  6.5 0.0 copy-start.2
  6.5 0.0 reduce-scatter.2.cloned.1.call-start
  6.5 4.5 %fusion.13 = f32[1728,512]{1,0:T(8,128)} fusion(bf16[1728,432]{0,1:T(8,128)(2,1)} %param.11, bf16[432,512]{1,0:T(8,128)(2,1)} %param.13), kind=kOutput, calls=%fused_computation.21 | convolution fusion | flops 764411904 | bytes 5474304 | tf_op jit(solution)/shard_map/dot_general | solution.py:13
  11.1 0.0 copy-done.1
  11.1 0.0 copy-done.2
  11.1 1.5 fusion.14
  12.5 168.2 %all-reduce.3 = (bf16[640,512]{1,0:T(8,128)(2,1)S(1)}, bf16[1728,512]{1,0:T(8,128)(2,1)}) all-reduce(f32[640,512]{1,0:T(8,128)} %fusion.14, f32[1728,512]{1,0:T(8,128)} %fusion.13), channel_id=1, replica_groups=mesh['ex'=32,'lay'=8] {'ex'}, use_global_device_ids=true, to_apply=%region_2.0 | all-reduce | flops 1212416 | bytes 7274496 | tf_op jit(solution)/shard_map/psum | solution.py:15
  180.7 0.0 copy-done
  180.7 0.0 copy-start.3
  180.7 1.8 convolution_bitcast_fusion
  182.6 0.0 copy-done.3
  182.6 6.3 %convolution_bitcast_fusion.1 = f32[512,1,2048]{2,0,1:T(8,128)S(1)} fusion(bf16[2048,1728]{0,1:T(8,128)(2,1)} %param.9, bf16[1728,512]{1,0:T(8,128)(2,1)S(1)} %copy-done.3), kind=kOutput, calls=%fused_computation.2 | convolution fusion | flops 3623878656 | bytes 13041664 | tf_op jit(solution)/shard_map/tf,fc->ct/dot_general | solution.py:21
  188.9 3.8 %pad_maximum_fusion = f32[512,2,2048]{2,0,1:T(8,128)} fusion(f32[512,1,2048]{2,0,1:T(8,128)S(1)} %convolution_bitcast_fusion, f32[512,1,2048]{2,0,1:T(8,128)S(1)} %convolution_bitcast_fusion.1), kind=kLoop, calls=%fused_computation | loop fusion | flops 2097152 | bytes 16777216 | tf_op jit(solution)/shard_map/stack | solution.py:24
  192.7 0.0 copy-start.5
  192.7 0.0 copy-start.6
  192.7 0.0 copy-start.4
  192.7 0.0 reduce-scatter.2.cloned.1.call-update
  192.8 0.6 copy-done.5
  193.4 0.2 reduce-window.8
  193.6 0.0 copy-done.6
  193.6 0.6 dynamic-slice
  194.8 0.0 copy-done.4
  194.8 0.2 dynamic-update-slice
  195.1 25.0 %all-reduce = s32[64]{0:T(128)S(1)} all-reduce(s32[64]{0:T(128)S(1)} %dynamic-update-slice), channel_id=1, replica_groups=mesh['ex'=32,'lay'=8] {'ex'}, use_global_device_ids=true, to_apply=%add | all-reduce | flops 64 | bytes 512
  220.1 34.6 %reduce-scatter.2.cloned.1.call-done = f32[64,2,2048]{2,0,1:T(8,128)} async-done(((f32[512,2,2048]{2,0,1:T(8,128)}), f32[64,2,2048]{2,0,1:T(8,128)}) %reduce-scatter.2.cloned.1.call-update) | async-done | bytes 1048592 | tf_op jit(solution)/shard_map/reduce_scatter | solution.py:23
  254.7 1.3 fusion.3
  256.0 0.2 fusion.1
  256.2 43.0 %all-gather = f32[32,2,2]{2,1,0:T(2,128)S(1)} all-gather(f32[1,2,2]{2,1,0:T(2,128)S(1)} %fusion.1), channel_id=1, replica_groups=mesh['ex'=32,'lay'=8] {'ex'}, dimensions={0}, use_global_device_ids=true | all-gather | bytes 528 | tf_op jit(solution)/shard_map/all_gather | solution.py:44
  299.1 0.8 fusion.9
  (3 shorter events, 0.0 us)
Async XLA Ops:
  6.5 174.2 %copy-start = (bf16[2048,640]{1,0:T(8,128)(2,1)S(1)}, bf16[2048,640]{1,0:T(8,128)(2,1)}, u32[]{:S(2)}) copy-start(bf16[2048,640]{1,0:T(8,128)(2,1)} %param.8) | copy-start | bytes 7864324
  6.5 4.5 %copy-start.1 = (bf16[640,160]{0,1:T(8,128)(2,1)S(1)}, bf16[640,160]{0,1:T(8,128)(2,1)}, u32[]{:S(2)}) copy-start(bf16[640,160]{0,1:T(8,128)(2,1)} %param.10) | copy-start | bytes 614404
  6.5 4.5 %copy-start.2 = (bf16[160,512]{1,0:T(8,128)(2,1)S(1)}, bf16[160,512]{1,0:T(8,128)(2,1)}, u32[]{:S(2)}) copy-start(bf16[160,512]{1,0:T(8,128)(2,1)} %param.12) | copy-start | bytes 491524
  6.5 248.1 %reduce-scatter.2.cloned.1.call-start = ((), (), s32[]{:S(2)}) async-start(), calls=%async_computation.1 | async-start | bytes 9437184 | tf_op jit(solution)/shard_map/reduce_scatter | solution.py:23
  180.7 1.8 copy-start.3
  192.7 0.7 copy-start.5
  192.7 0.8 copy-start.6
  192.7 2.1 copy-start.4
Sparse Core Ops, SparseCore 0:
  192.9 61.7 reduce-scatter.1
where the time goes:
time: 307 us
  blocking collectives  236 us (77%)
  waiting for transfers between devices  34.6 us (11%)
  matrix products  15.1 us (5%)
  between operations  14.1 us (5%)
  other arithmetic  5.26 us (2%)
    psum x1, blocking collectives, shards(): grad_sum, act_sum = lax.psum((grad_part, act_part), 'ex')  168 us
    all_gather x1, blocking collectives, shards(): lax.all_gather(packed, 'ex', axis=0, tiled=True)  43 us
    reduce_scatter x1, waiting for transfers between devices, shards(): lax.psum_scatter(jnp.stack([grad_part, act_part], axis=1), 'lay', scatter...  34.6 us
    unnamed x1, blocking collectives  25 us
    dot_general x1, matrix products, shards(): jnp.einsum('tf,fc->ct', grads, grad_rot, preferred_element_type=jnp.float32)  6.33 us
  transfers between devices with their start and end apart: 1, of which 1 were waited for; matrix products, arithmetic and copies ran while one was open for 0% of the time, Pallas kernels for 0%

commit v1 on v0

v1 whole, which is shorter than its diff:
```python
import functools
import math

import jax
import jax.numpy as jnp
from jax import lax
from jax.experimental import pallas as pl
from jax.experimental.pallas import tpu as pltpu
from jax.sharding import PartitionSpec as P

RANK = 32
LMAX = 1024
NY, NZ, NX = 4, 8, 4
W = 128
MESH = pl.DeviceIdType.MESH
F32, BF16 = jnp.float32, jnp.bfloat16


class Plan:
    def __init__(self):
        self.tasks = []
        self.messages = 0

    def message(self, count=1):
        first = self.messages
        self.messages += count
        return first

    def task(self, emit, cost, after=(), arrivals=(), sends=(), rank=0):
        self.tasks.append((emit, cost, tuple(after), tuple(arrivals), tuple(sends), rank))
        return len(self.tasks) - 1

    def order(self):
        now, done, arrived, link_free, left, out = 0.0, {}, {}, {}, list(range(len(self.tasks))), []
        while left:
            best = None
            for at in left:
                _, cost, after, arrivals, _, rank = self.tasks[at]
                if any(a not in done for a in after) or any(m not in arrived for m in arrivals):
                    continue
                start = max([now] + [arrived[m] for m in arrivals])
                key = (start, rank, at)
                if best is None or key < best:
                    best = key
            start, _, at = best
            _, cost, _, _, sends, _ = self.tasks[at]
            now = start + cost
            done[at] = now
            for number, link, size in sends:
                rate, latency = (0.3, 0.8) if link == "core" else (0.06, 1.8)
                begin = max(now, link_free.get(link, 0.0))
                link_free[link] = begin + size / rate * 1e-3
                arrived[number] = link_free[link] + latency
            left.remove(at)
            out.append(at)
        return out


def kernel(lens, dest, acts, grads, abasis, gbasis, aquery, gquery, out,
           xa, xg, ba, bg, qa, qg, part, fin, rsbig, rssmall, acc, pown, psend, precv, xr, tsum, laybuf, exbuf,
           ins, ss, rs):
    ex, lay = lax.axis_index("ex"), lax.axis_index("lay")
    y, z = lax.div(ex, NZ), lax.rem(ex, NZ)
    x, c = lax.div(lay, 2), lax.rem(lay, 2)
    nf, na = gbasis.shape[0], abasis.shape[0]
    chunks = part.shape[0]
    rows = part.shape[1]
    tok = acts.shape[0]
    half = tok // 2
    quarter = half // NX
    small = rows // (NY * NZ)

    def wrap(v, n):
        return lax.rem(v + n, n)

    def yz(dy, dz):
        return (wrap(y + dy, NY) * NZ + wrap(z + dz, NZ), lay)

    def across(dx, dc=0):
        return (ex, wrap(x + dx, NX) * 2 + wrap(c + dc, 2))

    def copy(number, src, dst, device):
        return pltpu.make_async_remote_copy(src, dst, ss.at[number], rs.at[number], device_id=device, device_id_type=MESH)

    loads = [(gquery, qg), (gbasis, bg), (aquery, qa), (abasis, ba), (grads, xg), (acts, xa)]
    local = [pltpu.make_async_copy(src, dst, ins.at[i]) for i, (src, dst) in enumerate(loads)]
    for one in local:
        one.start()

    barrier = pltpu.get_barrier_semaphore()
    partners = [yz(i // NZ, i % NZ) for i in range(1, NY * NZ)] + [across(i // 2, i % 2) for i in range(1, 2 * NX)]
    for device in partners:
        pl.semaphore_signal(barrier, inc=1, device_id=device, device_id_type=MESH)

    plan = Plan()
    sent = []

    def post(number, src, dst, device):
        one = copy(number, src, dst, device)
        one.start()
        sent.append(one)

    def rotate(pair):
        def emit():
            if pair == 0:
                for one in local[:4]:
                    one.wait()
            cols = pl.ds(pair * 2 * W, 2 * W)

            def block(basis, query, size, count, base):
                def body(i, _):
                    at = pl.multiple_of(i * size, 16)
                    r = jnp.dot(basis[pl.ds(at, size), :], query[:, cols], preferred_element_type=F32)
                    to = pl.ds(pl.multiple_of(base + i * size, 16), size)
                    part[2 * pair, to, :] = r[:, :W]
                    part[2 * pair + 1, to, :] = r[:, W:]
                    return 0

                lax.fori_loop(0, count, body, 0)

            block(bg, qg, nf // 6, 6, 0)
            block(ba, qa, na // 2, 2, nf)
            for j in (2 * pair, 2 * pair + 1):
                part[j, nf + na :, :] = jnp.zeros((rows - nf - na, W), F32)
            if pair == 0:
                pl.semaphore_wait(barrier, len(partners))

        return emit

    rotated = [plan.task(rotate(0), 3.0)]
    rotated.append(plan.task(rotate(1), 0.7, after=rotated, rank=0))

    def reach(axis, step):
        return yz(step, 0) if axis == "y" else yz(0, step)

    def rs_chain(j, axis, sign, hops, src, buf, size, after, rank):
        pos, n = (y, NY) if axis == "y" else (z, NZ)
        number = [plan.message() for _ in range(hops)]
        prev = after
        for s in range(hops):
            def emit(s=s):
                piece = src(wrap(pos + sign * (hops - s), n))
                if s:
                    copy(number[s - 1], piece, buf(s - 1), reach(axis, sign)).wait_recv()
                    buf(s - 1)[...] += piece[...]
                    piece = buf(s - 1)
                post(number[s], piece, buf(s), reach(axis, sign))

            at = plan.task(emit, 0.15 if s else 0.05, after=prev, arrivals=[number[s - 1]] if s else [],
                           sends=[(number[s], axis + str(sign), size * W * 4e-3)], rank=rank)
            prev = [at]
        return number[-1], buf(hops - 1)

    def ag_chain(j, axis, sign, hops, ref, size, after, rank):
        pos, n = (y, NY) if axis == "y" else (z, NZ)
        number = [plan.message() for _ in range(hops)]
        prev = after
        for s in range(hops):
            def emit(s=s):
                if s:
                    mine = ref(wrap(pos - sign * s, n))
                    copy(number[s - 1], mine, mine, reach(axis, sign)).wait_recv()
                piece = ref(wrap(pos - sign * s, n))
                post(number[s], piece, piece, reach(axis, sign))

            at = plan.task(emit, 0.05, after=prev, arrivals=[number[s - 1]] if s else [],
                           sends=[(number[s], axis + str(sign), size * W * 2e-3)], rank=rank)
            prev = [at]

        def last():
            mine = ref(wrap(pos - sign * hops, n))
            copy(number[-1], mine, mine, reach(axis, sign)).wait_recv()

        return prev, number[-1], last

    def slab(ref, at, size):
        return ref.at[pl.ds(pl.multiple_of(at, 16), size), :]

    ready = []
    for j in range(chunks):
        zfirst = j % 2 == 0
        flip = 1 if j % 4 < 2 else -1
        begin = [rotated[j // 2]]
        rank = j
        if zfirst:
            mid = small * NY
            ends = [
                rs_chain(j, "z", flip, NZ // 2, lambda d, j=j: slab(part.at[j], d * mid, mid),
                         lambda s, j=j: rsbig.at[j, s], mid, begin, rank),
                rs_chain(j, "z", -flip, NZ // 2 - 1, lambda d, j=j: slab(part.at[j], d * mid, mid),
                         lambda s, j=j: rsbig.at[j, NZ // 2 + s], mid, begin, rank),
            ]

            def middle(j=j, ends=ends):
                for number, buf in ends:
                    copy(number, buf, buf, yz(0, 1)).wait_recv()
                acc[j, : small * NY, :] = slab(part.at[j], z * small * NY, small * NY)[...] + ends[0][1][...] + ends[1][1][...]

            at = plan.task(middle, 0.2, after=begin, arrivals=[n for n, _ in ends], rank=rank)
            ends2 = [
                rs_chain(j, "y", flip, NY // 2, lambda d, j=j: slab(acc.at[j], d * small, small),
                         lambda s, j=j: rssmall.at[j, s], small, [at], rank),
                rs_chain(j, "y", -flip, NY // 2 - 1, lambda d, j=j: slab(acc.at[j], d * small, small),
                         lambda s, j=j: rssmall.at[j, NY // 2 + s], small, [at], rank),
            ]

            def finish(j=j, ends2=ends2):
                for number, buf in ends2:
                    copy(number, buf, buf, yz(1, 0)).wait_recv()
                total = slab(acc.at[j], y * small, small)[...] + ends2[0][1][...] + ends2[1][1][...]
                slab(fin.at[j], z * small * NY + y * small, small)[...] = total.astype(BF16)

            at = plan.task(finish, 0.1, after=[at], arrivals=[n for n, _ in ends2], rank=rank)
            inner = [ag_chain(j, "y", s, h, lambda d, j=j: slab(fin.at[j], z * small * NY + d * small, small), small, [at], rank)
                     for s, h in ((flip, NY // 2), (-flip, NY // 2 - 1))]
            outer_of = [("z", flip, NZ // 2, lambda d, j=j: slab(fin.at[j], d * small * NY, small * NY), small * NY),
                        ("z", -flip, NZ // 2 - 1, lambda d, j=j: slab(fin.at[j], d * small * NY, small * NY), small * NY)]
        else:
            wide = small * NZ
            part_rows = wide // 2
            ends = []
            for k, sgn in ((0, flip), (1, -flip)):
                src = lambda d, j=j, k=k: slab(part.at[j], d * wide + k * part_rows, part_rows)
                ends.append(rs_chain(j, "y", sgn, NY // 2, src, lambda s, j=j, k=k: rsbig.at[j, 3 * k + s], part_rows, begin, rank))
                ends.append(rs_chain(j, "y", -sgn, NY // 2 - 1, src, lambda s, j=j, k=k: rsbig.at[j, 3 * k + 2 + s], part_rows, begin, rank))

            def middle(j=j, ends=ends, wide=wide, part_rows=part_rows):
                for number, buf in ends:
                    copy(number, buf, buf, yz(1, 0)).wait_recv()
                for k in (0, 1):
                    acc[j, k * part_rows : (k + 1) * part_rows, :] = (
                        slab(part.at[j], y * wide + k * part_rows, part_rows)[...] + ends[2 * k][1][...] + ends[2 * k + 1][1][...])

            at = plan.task(middle, 0.3, after=begin, arrivals=[n for n, _ in ends], rank=rank)
            ends2 = [
                rs_chain(j, "z", flip, NZ // 2, lambda d, j=j: slab(acc.at[j], d * small, small),
                         lambda s, j=j: rssmall.at[j, s], small, [at], rank),
                rs_chain(j, "z", -flip, NZ // 2 - 1, lambda d, j=j: slab(acc.at[j], d * small, small),
                         lambda s, j=j: rssmall.at[j, NZ // 2 + s], small, [at], rank),
            ]

            def finish(j=j, ends2=ends2, wide=wide):
                for number, buf in ends2:
                    copy(number, buf, buf, yz(0, 1)).wait_recv()
                total = slab(acc.at[j], z * small, small)[...] + ends2[0][1][...] + ends2[1][1][...]
                slab(fin.at[j], y * wide + z * small, small)[...] = total.astype(BF16)

            at = plan.task(finish, 0.1, after=[at], arrivals=[n for n, _ in ends2], rank=rank)
            inner = [ag_chain(j, "z", s, h, lambda d, j=j, wide=wide: slab(fin.at[j], y * wide + d * small, small), small, [at], rank)
                     for s, h in ((flip, NZ // 2), (-flip, NZ // 2 - 1))]
            outer_of = []
            for k, sgn in ((0, flip), (1, -flip)):
                ref = lambda d, j=j, k=k, wide=wide, part_rows=part_rows: slab(fin.at[j], d * wide + k * part_rows, part_rows)
                outer_of.append(("y", sgn, NY // 2, ref, part_rows))
                outer_of.append(("y", -sgn, NY // 2 - 1, ref, part_rows))

        def joined(inner=inner):
            for _, _, last in inner:
                last()

        at = plan.task(joined, 0.02, after=[a for prev, _, _ in inner for a in prev], arrivals=[n for _, n, _ in inner], rank=rank)
        outer = [ag_chain(j, a, s, h, ref, size, [at], rank) for a, s, h, ref, size in outer_of]

        def complete(outer=outer, j=j):
            for _, _, last in outer:
                last()
            if j == 0:
                for one in local[4:]:
                    one.wait()

        ready.append(plan.task(complete, 0.02, after=[a for prev, _, _ in outer for a in prev], arrivals=[n for _, n, _ in outer], rank=rank))

    size4 = quarter * W * 4e-3
    scored = []
    for j in range(chunks):
        rank = 10 + j
        to_core = plan.message(NX)

        def project(rows_at, store, j=j):
            token = pl.ds(pl.multiple_of(rows_at, 16), quarter)
            store(jnp.dot(xg[token, :], fin[j, :nf, :], preferred_element_type=F32),
                  jnp.dot(xa[token, :], fin[j, nf : nf + na, :], preferred_element_type=F32))

        def theirs(j=j, to_core=to_core, project=project):
            def body(i, _):
                q = lax.rem(x + 2 + i, NX)

                def store(g, a):
                    psend[j, i, 0] = g
                    psend[j, i, 1] = a

                project((1 - c) * half + q * quarter, store)
                copy(to_core + i, psend.at[j, i], precv.at[j, i], across(0, 1)).start()
                return 0

            lax.fori_loop(0, NX, body, 0)
            for i in range(NX):
                sent.append(copy(to_core + i, psend.at[j, i], precv.at[j, i], across(0, 1)))

        def ours(j=j, project=project):
            def body(i, _):
                q = lax.rem(x + 2 + i, NX)

                def store(g, a):
                    pown[j, i, 0] = g
                    pown[j, i, 1] = a

                project(c * half + q * quarter, store)
                return 0

            lax.fori_loop(0, NX, body, 0)

        at = plan.task(theirs, 1.3, after=[ready[j]], sends=[(to_core + i, "core", 2 * size4) for i in range(NX)], rank=rank)
        at = plan.task(ours, 1.3, after=[at], rank=rank)
        m = [plan.message() for _ in range(6)]

        def pair_sum(i, j=j, to_core=to_core):
            copy(to_core + i, psend.at[j, i], precv.at[j, i], across(0, 1)).wait_recv()
            pown[j, i] += precv[j, i]

        def far(j=j, m=m, pair_sum=pair_sum):
            pair_sum(0)
            post(m[0], pown.at[j, 0, 0], xr.at[j, 0], across(1))
            post(m[1], pown.at[j, 0, 1], xr.at[j, 1], across(-1))

        def near(j=j, m=m, pair_sum=pair_sum):
            pair_sum(1)
            pair_sum(3)
            post(m[2], pown.at[j, 1, 0], xr.at[j, 2], across(-1))
            post(m[3], pown.at[j, 3, 1], xr.at[j, 3], across(1))

        def relay(j=j, m=m):
            copy(m[0], xr.at[j, 0], xr.at[j, 0], across(1)).wait_recv()
            pown[j, 3, 0] += xr[j, 0]
            post(m[4], pown.at[j, 3, 0], xr.at[j, 4], across(1))
            copy(m[1], xr.at[j, 1], xr.at[j, 1], across(-1)).wait_recv()
            pown[j, 1, 1] += xr[j, 1]
            post(m[5], pown.at[j, 1, 1], xr.at[j, 5], across(-1))

        def score(j=j, m=m, pair_sum=pair_sum):
            pair_sum(2)
            for k in (2, 3, 4, 5):
                copy(m[k], xr.at[j, k], xr.at[j, k], across(1)).wait_recv()
            g = pown[j, 2, 0] + xr[j, 2] + xr[j, 4]
            a = pown[j, 2, 1] + xr[j, 3] + xr[j, 5]
            product = g * a
            token = c * half + x * quarter + lax.broadcasted_iota(jnp.int32, (quarter, W), 0)
            first, both = lens[0], lens[0] + lens[1]
            s0 = jnp.sum(jnp.where(token < first, product, 0.0), axis=0, keepdims=True)
            s1 = jnp.sum(jnp.where((token >= first) & (token < both), product, 0.0), axis=0, keepdims=True)
            row = lax.broadcasted_iota(jnp.int32, (8, W), 0)
            tsum[:, j * W : (j + 1) * W] = jnp.where(row == 0, s0, jnp.where(row == 1, s1, 0.0))

        a1 = plan.task(far, 0.2, after=[at], arrivals=[to_core], sends=[(m[0], "x1", size4), (m[1], "x-1", size4)], rank=rank)
        a2 = plan.task(near, 0.3, after=[a1], arrivals=[to_core + 1, to_core + 3],
                       sends=[(m[2], "x-1", size4), (m[3], "x1", size4)], rank=rank)
        a3 = plan.task(relay, 0.2, after=[a2], arrivals=[m[0], m[1]], sends=[(m[4], "x1", size4), (m[5], "x-1", size4)], rank=rank)
        scored.append(plan.task(score, 0.3, after=[a3], arrivals=[m[2], m[3], m[4], m[5], to_core + 2], rank=rank))

    for at in plan.order():
        plan.tasks[at][0]()

    used = plan.messages
    columns = chunks * W
    group = lax.broadcasted_iota(jnp.int32, (columns, W), 0) // RANK
    pick = (group == lax.broadcasted_iota(jnp.int32, (columns, W), 1)).astype(F32)
    laybuf[0] = jnp.dot(tsum[...], pick, precision=lax.Precision.HIGHEST, preferred_element_type=F32)
    for i in range(1, 2 * NX):
        post(used + i, laybuf.at[0], laybuf.at[i], across(i // 2, i % 2))
    total = laybuf[0]
    for i in range(1, 2 * NX):
        copy(used + i, laybuf.at[i], laybuf.at[i], across(i // 2, i % 2)).wait_recv()
        total = total + laybuf[i]
    used += 2 * NX
    factor = 1.0 / math.sqrt(LMAX * RANK)
    row = lax.broadcasted_iota(jnp.int32, (8, W), 0)
    lane = lax.broadcasted_iota(jnp.int32, (8, W), 1)
    named = jnp.where(row == 0, dest[0], jnp.where(row == 1, dest[1], -1)).astype(F32)
    exbuf[0] = jnp.where(lane == 16, named, total * factor)
    for i in range(1, NY * NZ):
        post(used + i, exbuf.at[0], exbuf.at[i], yz(i // NZ, i % NZ))
    for i in range(1, NY * NZ):
        copy(used + i, exbuf.at[i], exbuf.at[i], yz(i // NZ, i % NZ)).wait_recv()
    every = exbuf[...].reshape(NY * NZ * 8, W)
    target = every[:, 16:17]
    picked = []
    for r in range(2):
        hit = target == (2 * ex + r).astype(F32)
        one = jnp.sum(jnp.where(hit, every, 0.0), axis=0, keepdims=True)
        for k in range(2):
            at = lax.broadcasted_iota(jnp.int32, (1, W), 1) == 2 * lay + k
            picked.append(jnp.sum(jnp.where(at, one, 0.0), axis=1, keepdims=True))
    row = lax.broadcasted_iota(jnp.int32, (2, 2), 0)
    lane = lax.broadcasted_iota(jnp.int32, (2, 2), 1)
    out[...] = jnp.where(row == 0, jnp.where(lane == 0, picked[0], picked[1]), jnp.where(lane == 0, picked[2], picked[3]))

    for one in sent:
        one.wait_send()


def shards(acts, grads, act_basis, grad_basis, act_query, grad_query, lengths, destination):
    tok, na = acts.shape
    nf = grads.shape[1]
    columns = grad_query.shape[1]
    chunks = columns // W
    rows = -(-(nf + na) // (16 * NY * NZ)) * 16 * NY * NZ
    small = rows // (NY * NZ)
    quarter = tok // 8
    any_ = pl.BlockSpec(memory_space=pl.ANY)
    smem = pl.BlockSpec(memory_space=pltpu.SMEM)
    messages = 512
    return pl.pallas_call(
        kernel,
        out_shape=jax.ShapeDtypeStruct((2, 2), F32),
        in_specs=[smem, smem] + [any_] * 6,
        out_specs=pl.BlockSpec(memory_space=pltpu.VMEM),
        scratch_shapes=[
            pltpu.VMEM(acts.shape, BF16),
            pltpu.VMEM(grads.shape, BF16),
            pltpu.VMEM(act_basis.shape, BF16),
            pltpu.VMEM(grad_basis.shape, BF16),
            pltpu.VMEM(act_query.shape, BF16),
            pltpu.VMEM(grad_query.shape, BF16),
            pltpu.VMEM((chunks, rows, W), F32),
            pltpu.VMEM((chunks, rows, W), BF16),
            pltpu.VMEM((chunks, 7, small * NY, W), F32),
            pltpu.VMEM((chunks, 7, small, W), F32),
            pltpu.VMEM((chunks, small * NZ, W), F32),
            pltpu.VMEM((chunks, NX, 2, quarter, W), F32),
            pltpu.VMEM((chunks, NX, 2, quarter, W), F32),
            pltpu.VMEM((chunks, NX, 2, quarter, W), F32),
            pltpu.VMEM((chunks, 6, quarter, W), F32),
            pltpu.VMEM((8, columns), F32),
            pltpu.VMEM((2 * NX, 8, W), F32),
            pltpu.VMEM((NY * NZ, 8, W), F32),
            pltpu.SemaphoreType.DMA((6,)),
            pltpu.SemaphoreType.DMA((messages,)),
            pltpu.SemaphoreType.DMA((messages,)),
        ],
        compiler_params=pltpu.CompilerParams(collective_id=0, has_side_effects=True, vmem_limit_bytes=60 << 20),
        name="influence",
    )(lengths, destination, acts, grads, act_basis, grad_basis, act_query, grad_query)


def solution(mesh):
    return jax.shard_map(
        shards,
        mesh=mesh,
        in_specs=(
            P("ex", "lay"),
            P("ex", "lay"),
            P("lay", "ex"),
            P("lay", "ex"),
            P("ex", None),
            P("ex", None),
            P("ex"),
            P("ex"),
        ),
        out_specs=P("ex", "lay"),
        check_vma=False,
    )
```

time: 307 us -> 147 us (0.48)
  blocking collectives: 236 us -> 0 us
  Pallas kernels: 0 us -> 129 us
  waiting for transfers between devices: 34.6 us -> 0 us
  local copies, waits for them, and re-layouts: 1.47 us -> 16.8 us
  matrix products: 15.1 us -> 0 us
  between operations: 14.1 us -> 0.01 us
  other arithmetic: 5.26 us -> 0 us
    psum x1 -> x0, blocking collectives: 168 us -> none  [shards(): grad_sum, act_sum = lax.psum((grad_part, act_part), 'ex')]
    pallas_call x0 -> x1, Pallas kernels: none -> 129 us  [shards(): pl.pallas_call(kernel, out_shape=jax.ShapeDtypeStruct((2, 2), F32), in_sp...]
    all_gather x1 -> x0, blocking collectives: 43 us -> none  [shards(): lax.all_gather(packed, 'ex', axis=0, tiled=True)]
    reduce_scatter x1 -> x0, waiting for transfers between devices: 34.6 us -> none  [shards(): lax.psum_scatter(jnp.stack([grad_part, act_part], axis=1), 'lay', scatter...]
    unnamed x1 -> x0, blocking collectives: 25 us -> none
    unnamed x17 -> x4, local copies, waits for them, and re-layouts: 1.47 us -> 16.8 us
    dot_general x6 -> x0, matrix products: 15.1 us -> none  [the longest x1 6.33 us: shards(): jnp.einsum('tf,fc->ct', grads, grad_rot, preferred_element_type=jnp.float32)]
    another operation x2 -> x0, other arithmetic: 3.98 us -> none  [the longest x1 3.8 us: shards(): jnp.stack([grad_part, act_part], axis=1)]
  transfers between devices with their start and end apart: 1 -> 0, of which waited for: 1 -> 0; matrix products, arithmetic and copies ran while one was open for 0% -> 0% of each run, Pallas kernels for 0% -> 0%
where the time goes in v1:
time: 147 us; the launch traced here: 146 us
  Pallas kernels  129 us (88%)
  local copies, waits for them, and re-layouts  16.8 us (11%)
    pallas_call x1, Pallas kernels, shards(): pl.pallas_call(kernel, out_shape=jax.ShapeDtypeStruct((2, 2), F32), in_sp...  129 us
    unnamed x4, local copies, waits for them, and re-layouts  16.8 us

profile of v1, /device:TPU:8, one launch (start us, length us, event | category | flops | bytes accessed | tf_op | source)
XLA Modules:
  0.0 145.7 jit_solution(3155372442493616702)
XLA Ops:
  0.0 1.9 %copy.10.abasis = bf16[640,160]{1,0:T(8,128)(2,1)} copy(bf16[640,160]{0,1:T(8,128)(2,1)} %param.10) | data formatting | bytes 409600 | tf_op args[2]
  1.9 3.7 %copy.11.gbasis = bf16[1728,432]{1,0:T(8,128)(2,1)} copy(bf16[1728,432]{0,1:T(8,128)(2,1)} %param.11) | data formatting | bytes 2985984 | tf_op args[3]
  5.6 10.0 %copy.9.grads = bf16[2048,1728]{1,0:T(8,128)(2,1)} copy(bf16[2048,1728]{0,1:T(8,128)(2,1)} %param.9) | data formatting | bytes 14155776 | tf_op args[1]
  15.6 128.8 %influence.1 = f32[2,2]{1,0:T(2,128)} custom-call(s32[2]{0:T(128)} %lens.1, s32[2]{0:T(128)} %dest.1, bf16[2048,640]{1,0:T(8,128)(2,1)} %acts.1, bf16[2048,1728]{1,0:T(8,128)(2,1)} %copy.9.grads, bf16[640,160]{1,0:T(8,128)(2,1)} %copy.10.abasis, bf16[1728,432]{1,0:T(8,128)(2,1)} %copy.11.gbasis, bf16[160,512]{1,0:T(8,128)(2,1)} %aquery.1, ...), custom_call_target="tpu_custom_call" | custom-call | tf_op jit(solution)/shard_map/influence/pallas_call | solution.py:412
  144.4 1.2 copy.13

commit v2 on v0

v2 whole, which is shorter than its diff:
```python
import functools
import math

import jax
import jax.numpy as jnp
from jax import lax
from jax.experimental import pallas as pl
from jax.experimental.pallas import tpu as pltpu
from jax.sharding import PartitionSpec as P

RANK = 32
LMAX = 1024
NY, NZ, NX = 4, 8, 4
W = 128
MESH = pl.DeviceIdType.MESH
F32, BF16 = jnp.float32, jnp.bfloat16


class Plan:
    def __init__(self):
        self.tasks = []
        self.messages = 0

    def message(self, count=1):
        first = self.messages
        self.messages += count
        return first

    def task(self, emit, cost, after=(), arrivals=(), sends=(), rank=0):
        self.tasks.append((emit, cost, tuple(after), tuple(arrivals), tuple(sends), rank))
        return len(self.tasks) - 1

    def order(self):
        now, done, arrived, link_free, left, out = 0.0, {}, {}, {}, list(range(len(self.tasks))), []
        while left:
            best = None
            for at in left:
                _, cost, after, arrivals, _, rank = self.tasks[at]
                if any(a not in done for a in after) or any(m not in arrived for m in arrivals):
                    continue
                start = max([now] + [arrived[m] for m in arrivals])
                key = (start, rank, at)
                if best is None or key < best:
                    best = key
            start, _, at = best
            _, cost, _, _, sends, _ = self.tasks[at]
            now = start + cost
            done[at] = now
            for number, link, size in sends:
                rate, latency = (0.3, 1.0) if link == "core" else (0.065, 4.0 if link == "zz" else 2.0)
                begin = max(now, link_free.get(link, 0.0))
                link_free[link] = begin + size / rate * 1e-3
                arrived[number] = link_free[link] + latency
            left.remove(at)
            out.append(at)
        return out


I16 = jnp.int16
TOP = 32000.0


def encode(value, scale):
    return jnp.floor(value * scale + 0.5).astype(jnp.int32).astype(I16)


def decode(code, unit):
    return code.astype(jnp.int32).astype(F32) * unit


def kernel(lens, dest, acts, grads, abasis, gbasis, aquery, gquery, out,
           xa, xg, ba, bg, qa, qg, qat, qgt, part, fin, ysend, ybuf, acc, zsend, zbuf, hy, hz, pown, psend, precv,
           xs, xr, tok, laybuf, exbuf, ins, ss, rs):
    ex, lay = lax.axis_index("ex"), lax.axis_index("lay")
    y, z = lax.div(ex, NZ), lax.rem(ex, NZ)
    x, c = lax.div(lay, 2), lax.rem(lay, 2)
    nf, na = gbasis.shape[1], abasis.shape[1]
    base = -(-nf // 128) * 128
    chunks, _, lanes = part.shape
    count = acts.shape[0]
    half = count // 2
    quarter = half // NX
    wide = lanes // NY
    short = W // NZ
    rows = W // 2

    def wrap(v, n):
        return lax.rem(v + n, n)

    def yz(dy, dz):
        return (wrap(y + dy, NY) * NZ + wrap(z + dz, NZ), lay)

    def across(dx, dc=0):
        return (ex, wrap(x + dx, NX) * 2 + wrap(c + dc, 2))

    def copy(number, src, dst, device):
        return pltpu.make_async_remote_copy(src, dst, ss.at[number], rs.at[number], device_id=device, device_id_type=MESH)

    loads = [(gquery, qg), (gbasis, bg), (aquery, qa), (abasis, ba), (grads, xg), (acts, xa)]
    local = [pltpu.make_async_copy(src, dst, ins.at[i]) for i, (src, dst) in enumerate(loads)]

    barrier = pltpu.get_barrier_semaphore()
    partners = [yz(0, 1), yz(0, -1), yz(1, 0), yz(-1, 0), across(1), across(-1), across(0, 1)]
    partners += [yz(2, 0)] + [yz(0, i) for i in range(2, NZ - 1)]
    for device in partners:
        pl.semaphore_signal(barrier, inc=1, device_id=device, device_id_type=MESH)
    for one in local:
        one.start()

    plan = Plan()
    sent = []

    def post(number, src, dst, device):
        one = copy(number, src, dst, device)
        one.start()
        sent.append(one)

    def fan(number, sends, whole):
        for src, dst, device in sends:
            copy(number, src, dst, device).start()
        sent.append(copy(number, whole, whole, yz(0, 1)))

    def landed(number, whole):
        copy(number, whole, whole, yz(0, 1)).wait_recv()

    def block(ref, row, height, lane, size):
        return ref.at[pl.ds(pl.multiple_of(row, 16), height), pl.ds(pl.multiple_of(lane, 128), size)]

    def piece(j, h, d):
        return block(part.at[j], h * rows, rows, d * wide, wide)

    def bounds(tile):
        return tile[0:1, 0:1], tile[0:1, 64:65]

    def spread(pair, d):
        lane = d * wide + lax.broadcasted_iota(jnp.int32, (1, wide), 1)
        return jnp.where(lane < base, pair[0], pair[1])

    hny, hnz = plan.message(), plan.message()
    state = {}

    def rot():
        local[0].wait()
        qgt[...] = qg[...].astype(F32).T.astype(BF16)
        local[2].wait()
        qat[...] = qa[...].astype(F32).T.astype(BF16)
        local[1].wait()
        largest = []
        for basis, query, size, at in ((bg, qgt, nf, 0), (ba, qat, na, base)):
            if size == na:
                local[3].wait()
            peak = jnp.zeros((1, 256), F32)
            for lo in range(0, size, 256):
                hi = min(lo + 256, size)
                r = jnp.dot(query[...], basis[:, lo:hi], preferred_element_type=F32)
                for j in range(chunks):
                    part[j, :, at + lo : at + hi] = r[j * W : (j + 1) * W]
                here = jnp.max(jnp.abs(r), axis=0, keepdims=True)
                if hi - lo < 256:
                    largest.append(jnp.max(here, axis=1, keepdims=True))
                else:
                    peak = jnp.maximum(peak, here)
            largest.append(jnp.max(peak, axis=1, keepdims=True))
        top_g, top_a = jnp.maximum(largest[0], largest[1]), jnp.maximum(largest[2], largest[3])
        for j in range(chunks):
            part[j, :, nf:base] = jnp.zeros((W, base - nf), F32)
            part[j, :, base + na :] = jnp.zeros((W, lanes - base - na), F32)
        lane = lax.broadcasted_iota(jnp.int32, (8, 128), 1)
        hy[0] = jnp.where(lane < 64, top_g, top_a)
        pl.semaphore_wait(barrier, len(partners))
        fan(hny, [(hy.at[0], hy.at[i], yz(i, 0)) for i in range(1, NY)], hy.at[1:NY])

    def scale_y():
        landed(hny, hy.at[1:NY])
        hz[0] = jnp.maximum(hy[0] + hy[1] + hy[2] + hy[3], 1e-30)
        fan(hnz, [(hz.at[0], hz.at[i], yz(0, i)) for i in range(1, NZ)], hz.at[1:NZ])
        state["unit"] = [b * (1.0 / TOP) for b in bounds(hz[0])]
        state["scale"] = [TOP / b for b in bounds(hz[0])]

    def scale_z():
        landed(hnz, hz.at[1:NZ])
        for i in range(1, NZ):
            state["unit", i] = [b * (1.0 / TOP) for b in bounds(hz[i])]

    begin = plan.task(rot, 4.0, sends=[(hny, "y0", 0.0)])
    begin = plan.task(scale_y, 0.5, after=[begin], arrivals=[hny], sends=[(hnz, "zz", 0.0)])
    begin2 = plan.task(scale_z, 0.5, after=[begin], arrivals=[hnz])

    ready = []
    for j in range(chunks):
        rank = j
        size = rows * wide * 2e-3
        signs = (1, -1)
        n = [[plan.message() for _ in range(3)] for _ in signs]

        def rs0(j=j, n=n):
            for h, sg in enumerate(signs):
                d = wrap(y + 2 * sg, NY)
                ysend[j, h, 0] = encode(piece(j, h, d)[...], spread(state["scale"], d))
                post(n[h][0], ysend.at[j, h, 0], ybuf.at[j, h, 0], yz(sg, 0))

        def rs1(j=j, n=n):
            for h, sg in enumerate(signs):
                d = wrap(y - sg, NY)
                ysend[j, h, 2] = encode(piece(j, h, d)[...], spread(state["scale"], d))
                post(n[h][2], ysend.at[j, h, 2], ybuf.at[j, h, 2], yz(-sg, 0))

        def rs2(h, sg, j=j, n=n):
            d = wrap(y + sg, NY)
            landed(n[h][0], ybuf.at[j, h, 0])
            total = piece(j, h, d)[...] + decode(ybuf[j, h, 0], spread(state["unit"], d))
            ysend[j, h, 1] = encode(total, spread(state["scale"], d))
            post(n[h][1], ysend.at[j, h, 1], ybuf.at[j, h, 1], yz(sg, 0))

        zn, zn2 = plan.message(), plan.message()

        def make_middle(zn=zn, j=j, n=n):
            def middle():
                unit, scale = spread(state["unit"], y), spread(state["scale"], y)
                for h in (0, 1):
                    landed(n[h][1], ybuf.at[j, h, 1])
                    landed(n[h][2], ybuf.at[j, h, 2])
                    total = piece(j, h, y)[...] + decode(ybuf[j, h, 1], unit) + decode(ybuf[j, h, 2], unit)
                    acc[j, h * rows : (h + 1) * rows, :] = total
                    zsend[j, h * rows : (h + 1) * rows, :] = encode(total, scale)
                fan(zn, [(block(zsend.at[j], wrap(z + i, NZ) * short, short, 0, wide), zbuf.at[j, i], yz(0, i))
                         for i in range(1, NZ)], zbuf.at[j, 1:NZ])

            return middle

        def finish(zn=zn, zn2=zn2, j=j):
            landed(zn, zbuf.at[j, 1:NZ])
            total = block(acc.at[j], z * short, short, 0, wide)[...]
            for i in range(1, NZ):
                total = total + decode(zbuf[j, i], spread(state["unit", i], y))
            mine = block(fin.at[j], z * short, short, y * wide, wide)
            mine[...] = total.astype(BF16)
            fan(zn2, [(mine, mine, yz(0, i)) for i in range(1, NZ)], zbuf.at[j, 1:NZ])

        a = [plan.message() for _ in range(6)]

        def fin_half(j, h, d):
            return block(fin.at[j], h * rows, rows, d * wide, wide)

        def ag0(zn2=zn2, a=a, j=j):
            landed(zn2, zbuf.at[j, 1:NZ])
            for h, sg in enumerate(signs):
                mine = fin_half(j, h, y)
                post(a[3 * h], mine, mine, yz(sg, 0))
            for h, sg in enumerate(signs):
                mine = fin_half(j, h, y)
                post(a[3 * h + 2], mine, mine, yz(-sg, 0))

        def ag1(h, sg, a=a, j=j):
            got = fin_half(j, h, wrap(y - sg, NY))
            landed(a[3 * h], got)
            post(a[3 * h + 1], got, got, yz(sg, 0))

        def complete(a=a, j=j):
            for h, sg in enumerate(signs):
                landed(a[3 * h + 1], fin_half(j, h, wrap(y - 2 * sg, NY)))
                landed(a[3 * h + 2], fin_half(j, h, wrap(y + sg, NY)))
            if j == 0:
                for one in local[4:]:
                    one.wait()

        t0 = plan.task(rs0, 0.3, after=[begin], sends=[(n[0][0], "y1", size), (n[1][0], "y-1", size)], rank=rank)
        t1 = plan.task(rs1, 0.3, after=[t0], sends=[(n[0][2], "y-1", size), (n[1][2], "y1", size)], rank=rank)
        t2 = []
        for h, sg in enumerate(signs):
            def rs2_of(h=h, sg=sg, rs2=rs2):
                rs2(h, sg)

            rs2_of.__name__ = "rs2"
            t2.append(plan.task(rs2_of, 0.3, after=[t0], arrivals=[n[h][0]], sends=[(n[h][1], "y%d" % sg, size)], rank=rank))
        t3 = plan.task(make_middle(), 1.0, after=t2 + [t1], arrivals=[n[0][1], n[0][2], n[1][1], n[1][2]],
                       sends=[(zn, "zz", 8 * short * wide * 2e-3)], rank=rank)
        t4 = plan.task(finish, 0.8, after=[t3, begin2], arrivals=[zn], sends=[(zn2, "zz", 8 * short * wide * 2e-3)], rank=rank)
        t5 = plan.task(ag0, 0.2, after=[t4], arrivals=[zn2], sends=[(a[0], "y1", size), (a[3], "y-1", size), (a[2], "y-1", size), (a[5], "y1", size)], rank=rank)
        t6 = []
        for h, sg in enumerate(signs):
            def ag1_of(h=h, sg=sg, ag1=ag1):
                ag1(h, sg)

            ag1_of.__name__ = "ag1"
            t6.append(plan.task(ag1_of, 0.1, after=[t5], arrivals=[a[3 * h]], sends=[(a[3 * h + 1], "y%d" % sg, size)], rank=rank))
        ready.append(plan.task(complete, 0.1, after=t6, arrivals=[a[1], a[2], a[4], a[5]], rank=rank))

    size4 = quarter * W * 4e-3
    size2 = quarter * (W + 16) * 2e-3
    tok[...] = jnp.zeros(tok.shape, F32)
    log2 = 1.0 / math.log(2.0)

    def pack(dst, value):
        bound = jnp.maximum(jnp.max(jnp.max(jnp.abs(value), axis=0, keepdims=True), axis=1, keepdims=True), 1e-30)
        power = jnp.ceil(jnp.log(bound) * log2)
        dst[:W, :] = encode(value, TOP * jnp.exp(power * (-1.0 / log2)))
        dst[W:, :] = jnp.broadcast_to(power, (16, quarter)).astype(jnp.int32).astype(I16)

    def unpack(src):
        power = src[W:, :].astype(jnp.int32).astype(F32)[0:1, 0:1]
        return decode(src[:W, :], jnp.exp(power * (1.0 / log2)) * (1.0 / TOP))

    for j in range(chunks):
        rank = 10 + j
        to_core = plan.message(NX)

        def project(at, store, j=j):
            token = pl.ds(pl.multiple_of(at, 128), quarter)
            store[0] = jnp.dot(fin[j, :, :nf], xg[:, token], preferred_element_type=F32)
            store[1] = lax.dot_general(fin[j, :, base : base + na], xa[token, :], (((1,), (1,)), ((), ())), preferred_element_type=F32)

        prev = [ready[j]]
        mine = []
        for i in range(NX):
            def theirs(i=i, j=j, to_core=to_core, project=project):
                project((1 - c) * half + lax.rem(x + 2 + i, NX) * quarter, psend.at[j, i])
                post(to_core + i, psend.at[j, i], precv.at[j, i], across(0, 1))

            prev = [plan.task(theirs, 0.5, after=prev, sends=[(to_core + i, "core", 2 * size4)], rank=rank)]
        for i in range(NX):
            def ours(i=i, j=j, project=project):
                project(c * half + lax.rem(x + 2 + i, NX) * quarter, pown.at[j, i])

            prev = [plan.task(ours, 0.5, after=prev, rank=rank)]
            mine.append(prev[0])
        m = [plan.message() for _ in range(6)]

        def pair_sum(i, j=j, to_core=to_core):
            landed(to_core + i, precv.at[j, i])
            pown[j, i] += precv[j, i]

        def send(k, value, dx, j=j, m=m):
            pack(xs.at[j, k], value)
            post(m[k], xs.at[j, k], xr.at[j, k], across(dx))

        def arrived(k, j=j, m=m):
            landed(m[k], xr.at[j, k])
            return unpack(xr.at[j, k])

        def far(j=j, send=send, pair_sum=pair_sum):
            pair_sum(0)
            send(0, pown[j, 0, 0], 1)
            send(1, pown[j, 0, 1], -1)

        def near(j=j, send=send, pair_sum=pair_sum):
            pair_sum(1)
            send(2, pown[j, 1, 0], -1)

        def near2(j=j, send=send, pair_sum=pair_sum):
            pair_sum(3)
            send(3, pown[j, 3, 1], 1)

        def relay(j=j, send=send, arrived=arrived):
            send(4, pown[j, 3, 0] + arrived(0), 1)
            send(5, pown[j, 1, 1] + arrived(1), -1)

        def score(j=j, arrived=arrived, pair_sum=pair_sum):
            pair_sum(2)
            g = pown[j, 2, 0] + arrived(2) + arrived(4)
            a = pown[j, 2, 1] + arrived(3) + arrived(5)
            tok[j * W // RANK : (j + 1) * W // RANK, :] = jnp.sum((g * a).reshape(W // RANK, RANK, quarter), axis=1)

        a1 = plan.task(far, 0.6, after=[mine[0]], arrivals=[to_core], sends=[(m[0], "x1", size2), (m[1], "x-1", size2)], rank=rank)
        a2 = plan.task(near, 0.4, after=[a1, mine[1]], arrivals=[to_core + 1], sends=[(m[2], "x-1", size2)], rank=rank)
        a2 = plan.task(near2, 0.4, after=[a2, mine[3]], arrivals=[to_core + 3], sends=[(m[3], "x1", size2)], rank=rank)
        a3 = plan.task(relay, 0.6, after=[a2], arrivals=[m[0], m[1]], sends=[(m[4], "x1", size2), (m[5], "x-1", size2)], rank=rank)
        plan.task(score, 0.6, after=[a3], arrivals=[m[2], m[3], m[4], m[5], to_core + 2], rank=rank)

    for at in plan.order():
        plan.tasks[at][0]()

    used = plan.messages
    row = lax.broadcasted_iota(jnp.int32, (8, quarter), 0)
    token = c * half + x * quarter + lax.broadcasted_iota(jnp.int32, (8, quarter), 1)
    lo = jnp.where(row == 0, 0, lens[0])
    hi = jnp.where(row == 0, lens[0], jnp.where(row == 1, lens[0] + lens[1], 0))
    member = ((token >= lo) & (token < hi)).astype(F32)
    laybuf[0] = lax.dot_general(member, tok[...], (((1,), (1,)), ((), ())), precision=lax.Precision.HIGHEST,
                                preferred_element_type=F32)
    fan(used, [(laybuf.at[0], laybuf.at[i], across(i // 2, i % 2)) for i in range(1, 2 * NX)], laybuf.at[1 : 2 * NX])
    landed(used, laybuf.at[1 : 2 * NX])
    total = laybuf[0]
    for i in range(1, 2 * NX):
        total = total + laybuf[i]
    factor = 1.0 / math.sqrt(LMAX * RANK)
    row = lax.broadcasted_iota(jnp.int32, (8, W), 0)
    lane = lax.broadcasted_iota(jnp.int32, (8, W), 1)
    named = jnp.where(row == 0, dest[0], jnp.where(row == 1, dest[1], -1)).astype(F32)
    exbuf[0] = jnp.where(lane == 16, named, total * factor)
    fan(used + 1, [(exbuf.at[0], exbuf.at[i], yz(i // NZ, i % NZ)) for i in range(1, NY * NZ)], exbuf.at[1 : NY * NZ])
    landed(used + 1, exbuf.at[1 : NY * NZ])
    every = exbuf[...].reshape(NY * NZ * 8, W)
    target = every[:, 16:17]
    picked = []
    for r in range(2):
        hit = target == (2 * ex + r).astype(F32)
        one = jnp.sum(jnp.where(hit, every, 0.0), axis=0, keepdims=True)
        for k in range(2):
            at = lax.broadcasted_iota(jnp.int32, (1, W), 1) == 2 * lay + k
            picked.append(jnp.sum(jnp.where(at, one, 0.0), axis=1, keepdims=True))
    row = lax.broadcasted_iota(jnp.int32, (2, 2), 0)
    lane = lax.broadcasted_iota(jnp.int32, (2, 2), 1)
    out[...] = jnp.where(row == 0, jnp.where(lane == 0, picked[0], picked[1]), jnp.where(lane == 0, picked[2], picked[3]))

    for one in sent:
        one.wait_send()


def shards(acts, grads, act_basis, grad_basis, act_query, grad_query, lengths, destination):
    grads, act_basis, grad_basis = grads.T, act_basis.T, grad_basis.T
    count, na = acts.shape
    nf = grads.shape[0]
    columns = grad_query.shape[1]
    chunks = columns // W
    tiles = -(-nf // 128) + -(-na // 128)
    lanes = -(-tiles // NY) * NY * 128
    short, wide = W // NZ, lanes // NY
    quarter = count // (2 * NX)
    any_ = pl.BlockSpec(memory_space=pl.ANY)
    smem = pl.BlockSpec(memory_space=pltpu.SMEM)
    messages = 2 + chunks * 24 + 2
    return pl.pallas_call(
        kernel,
        out_shape=jax.ShapeDtypeStruct((2, 2), F32),
        in_specs=[smem, smem] + [any_] * 6,
        out_specs=pl.BlockSpec(memory_space=pltpu.VMEM),
        scratch_shapes=[
            pltpu.VMEM(acts.shape, BF16),
            pltpu.VMEM(grads.shape, BF16),
            pltpu.VMEM(act_basis.shape, BF16),
            pltpu.VMEM(grad_basis.shape, BF16),
            pltpu.VMEM(act_query.shape, BF16),
            pltpu.VMEM(grad_query.shape, BF16),
            pltpu.VMEM(act_query.shape[::-1], BF16),
            pltpu.VMEM(grad_query.shape[::-1], BF16),
            pltpu.VMEM((chunks, W, lanes), F32),
            pltpu.VMEM((chunks, W, lanes), BF16),
            pltpu.VMEM((chunks, 2, 3, W // 2, wide), I16),
            pltpu.VMEM((chunks, 2, 3, W // 2, wide), I16),
            pltpu.VMEM((chunks, W, wide), F32),
            pltpu.VMEM((chunks, W, wide), I16),
            pltpu.VMEM((chunks, NZ, short, wide), I16),
            pltpu.VMEM((NY, 8, 128), F32),
            pltpu.VMEM((NZ, 8, 128), F32),
            pltpu.VMEM((chunks, NX, 2, W, quarter), F32),
            pltpu.VMEM((chunks, NX, 2, W, quarter), F32),
            pltpu.VMEM((chunks, NX, 2, W, quarter), F32),
            pltpu.VMEM((chunks, 6, W + 16, quarter), I16),
            pltpu.VMEM((chunks, 6, W + 16, quarter), I16),
            pltpu.VMEM((128, quarter), F32),
            pltpu.VMEM((2 * NX, 8, 128), F32),
            pltpu.VMEM((NY * NZ, 8, 128), F32),
            pltpu.SemaphoreType.DMA((6,)),
            pltpu.SemaphoreType.DMA((messages,)),
            pltpu.SemaphoreType.DMA((messages,)),
        ],
        compiler_params=pltpu.CompilerParams(collective_id=0, has_side_effects=True, vmem_limit_bytes=60 << 20),
        name="influence",
    )(lengths, destination, acts, grads, act_basis, grad_basis, act_query, grad_query)


def solution(mesh):
    return jax.shard_map(
        shards,
        mesh=mesh,
        in_specs=(
            P("ex", "lay"),
            P("ex", "lay"),
            P("lay", "ex"),
            P("lay", "ex"),
            P("ex", None),
            P("ex", None),
            P("ex"),
            P("ex"),
        ),
        out_specs=P("ex", "lay"),
        check_vma=False,
    )
```

time: 307 us -> 111 us (0.36)
  blocking collectives: 236 us -> 0 us
  Pallas kernels: 0 us -> 108 us
  waiting for transfers between devices: 34.6 us -> 0 us
  matrix products: 15.1 us -> 0 us
  between operations: 14.1 us -> 0.01 us
  other arithmetic: 5.26 us -> 0 us
    psum x1 -> x0, blocking collectives: 168 us -> none  [shards(): grad_sum, act_sum = lax.psum((grad_part, act_part), 'ex')]
    pallas_call x0 -> x1, Pallas kernels: none -> 108 us  [shards(): pl.pallas_call(kernel, out_shape=jax.ShapeDtypeStruct((2, 2), F32), in_sp...]
    all_gather x1 -> x0, blocking collectives: 43 us -> none  [shards(): lax.all_gather(packed, 'ex', axis=0, tiled=True)]
    reduce_scatter x1 -> x0, waiting for transfers between devices: 34.6 us -> none  [shards(): lax.psum_scatter(jnp.stack([grad_part, act_part], axis=1), 'lay', scatter...]
    unnamed x1 -> x0, blocking collectives: 25 us -> none
    dot_general x6 -> x0, matrix products: 15.1 us -> none  [the longest x1 6.33 us: shards(): jnp.einsum('tf,fc->ct', grads, grad_rot, preferred_element_type=jnp.float32)]
    another operation x2 -> x0, other arithmetic: 3.98 us -> none  [the longest x1 3.8 us: shards(): jnp.stack([grad_part, act_part], axis=1)]
  transfers between devices with their start and end apart: 1 -> 0, of which waited for: 1 -> 0; matrix products, arithmetic and copies ran while one was open for 0% -> 0% of each run, Pallas kernels for 0% -> 0%
where the time goes in v2:
time: 111 us; the launch traced here: 109 us
  Pallas kernels  108 us (97%)
  local copies, waits for them, and re-layouts  1.24 us (1%)
    pallas_call x1, Pallas kernels, shards(): pl.pallas_call(kernel, out_shape=jax.ShapeDtypeStruct((2, 2), F32), in_sp...  108 us

profile of v2, /device:TPU:8, one launch (start us, length us, event | category | flops | bytes accessed | tf_op | source)
XLA Modules:
  0.0 109.2 jit_solution(11085769491869498790)
XLA Ops:
  0.0 107.9 %influence.1 = f32[2,2]{1,0:T(2,128)} custom-call(s32[2]{0:T(128)} %lens.1, s32[2]{0:T(128)} %dest.1, bf16[2048,640]{1,0:T(8,128)(2,1)} %acts.1, bf16[1728,2048]{1,0:T(8,128)(2,1)} %bitcast.3, bf16[160,640]{1,0:T(8,128)(2,1)} %bitcast.5, bf16[432,1728]{1,0:T(8,128)(2,1)} %bitcast.4, bf16[160,512]{1,0:T(8,128)(2,1)} %aquery.1, bf16[432,512]{1,0:T(8,128)(2,1)} %gquery.1), custom_call_target="tpu_custom_call" | custom-call | tf_op jit(solution)/shard_map/influence/pallas_call | solution.py:423
  107.9 1.2 %copy.10 = f32[2,2]{1,0:T(2,128)} copy(f32[2,2]{1,0:T(2,128)} %influence.1) | data formatting | bytes 32

commit v3 on v2

v3 whole, which is shorter than its diff:
```python
import functools
import math

import jax
import jax.numpy as jnp
from jax import lax
from jax.experimental import pallas as pl
from jax.experimental.pallas import tpu as pltpu
from jax.sharding import PartitionSpec as P

RANK = 32
LMAX = 1024
NY, NZ, NX = 4, 8, 4
W = 128
MESH = pl.DeviceIdType.MESH
F32, BF16 = jnp.float32, jnp.bfloat16


class Plan:
    def __init__(self):
        self.tasks = []
        self.messages = 0
        self.groups = 0

    def message(self, count=1):
        first = self.messages
        self.messages += count
        return first

    def group(self):
        self.groups += 1
        return self.groups - 1

    def task(self, emit, cost, after=(), arrivals=(), sends=(), rank=0):
        self.tasks.append((emit, cost, tuple(after), tuple(arrivals), tuple(sends), rank))
        return len(self.tasks) - 1

    def order(self):
        now, done, arrived, link_free, left, out = 0.0, {}, {}, {}, list(range(len(self.tasks))), []
        while left:
            best = None
            for at in left:
                _, cost, after, arrivals, _, rank = self.tasks[at]
                if any(a not in done for a in after) or any(m not in arrived for m in arrivals):
                    continue
                start = max([now] + [arrived[m] for m in arrivals])
                key = (start, rank, at)
                if best is None or key < best:
                    best = key
            start, _, at = best
            _, cost, _, _, sends, _ = self.tasks[at]
            now = start + cost
            done[at] = now
            for number, link, size in sends:
                rate, latency = (0.3, 2.5) if link == "core" else (0.062, 4.0 if link[0] == "x" else 2.2)
                begin = max(now, link_free.get(link, 0.0))
                link_free[link] = begin + size / rate * 1e-3
                arrived[number] = link_free[link] + latency
            left.remove(at)
            out.append(at)
        return out


I16 = jnp.int16
TOP = 32000.0


def encode(value, scale):
    return jnp.floor(value * scale + 0.5).astype(jnp.int32).astype(I16)


def decode(code, unit):
    return code.astype(jnp.int32).astype(F32) * unit


def kernel(lens, dest, acts, grads, abasis, gbasis, aquery, gquery, out,
           xa, xg, ba, bg, qa, qg, qat, qgt, part, fin, ysend, ybuf, acc, zsend, zbuf, relayed, hy, hz, pfull, precv,
           xs, xr, pairs, exbuf, ins, ss, rs):
    ex, lay = lax.axis_index("ex"), lax.axis_index("lay")
    y, z = lax.div(ex, NZ), lax.rem(ex, NZ)
    x, c = lax.div(lay, 2), lax.rem(lay, 2)
    nf, na = gbasis.shape[1], abasis.shape[1]
    base = -(-nf // 128) * 128
    chunks, _, lanes = part.shape
    count = acts.shape[0]
    tile = count // 8
    own = W // 2
    each = own // NX
    wide = lanes // NY
    short = W // NZ
    rows = W // 2

    def wrap(v, n):
        return lax.rem(v + n, n)

    def yz(dy, dz):
        return (wrap(y + dy, NY) * NZ + wrap(z + dz, NZ), lay)

    def across(dx, dc=0):
        return (ex, wrap(x + dx, NX) * 2 + wrap(c + dc, 2))

    def copy(number, src, dst, device, group=0):
        return pltpu.make_async_remote_copy(src, dst, ss.at[group], rs.at[number], device_id=device, device_id_type=MESH)

    loads = [(gquery, qg), (gbasis, bg), (aquery, qa), (abasis, ba), (grads, xg), (acts, xa)]
    local = [pltpu.make_async_copy(src, dst, ins.at[i]) for i, (src, dst) in enumerate(loads)]

    barrier = pltpu.get_barrier_semaphore()
    partners = [yz(0, 1), yz(0, -1), yz(1, 0), yz(-1, 0), across(1), across(-1), across(0, 1)]
    partners += [yz(2, 0)] + [yz(0, i) for i in range(2, NZ - 1)]
    for device in partners:
        pl.semaphore_signal(barrier, inc=1, device_id=device, device_id_type=MESH)
    for one in local:
        one.start()

    plan = Plan()
    sent = []

    def group(whole):
        number = plan.group()
        sent.append(copy(0, whole, whole, yz(0, 1), number))
        return number

    def post(number, src, dst, device, of):
        copy(number, src, dst, device, of).start()

    def fan(number, sends, of):
        for src, dst, device in sends:
            copy(number, src, dst, device, of).start()

    def landed(number, whole):
        copy(number, whole, whole, yz(0, 1)).wait_recv()

    def block(ref, row, height, lane, size):
        return ref.at[pl.ds(pl.multiple_of(row, 16), height), pl.ds(pl.multiple_of(lane, 128), size)]

    def piece(j, h, d):
        return block(part.at[j], h * rows, rows, d * wide, wide)

    def bounds(tile):
        return tile[0:1, 0:1], tile[0:1, 64:65]

    def spread(pair, d):
        lane = d * wide + lax.broadcasted_iota(jnp.int32, (1, wide), 1)
        return jnp.where(lane < base, pair[0], pair[1])

    def arrange(rows_of):
        out_rows = []
        for j in range(chunks):
            for core in range(2):
                for at in range(NX):
                    for q in (4 * at + 2 * core, 4 * at + 2 * core + 1):
                        out_rows.append(rows_of[q * RANK + 8 * j : q * RANK + 8 * j + 8])
        return jnp.concatenate(out_rows, axis=0).astype(BF16)

    hny, hnz = plan.message(), plan.message()
    state = {}

    def rot():
        local[0].wait()
        qgt[...] = arrange(qg[...].astype(F32).T)
        local[2].wait()
        qat[...] = arrange(qa[...].astype(F32).T)
        local[1].wait()
        largest = []
        for basis, query, size, at in ((bg, qgt, nf, 0), (ba, qat, na, base)):
            if size == na:
                local[3].wait()
            peak = jnp.zeros((1, 256), F32)
            for lo in range(0, size, 256):
                hi = min(lo + 256, size)
                r = jnp.dot(query[...], basis[:, lo:hi], preferred_element_type=F32)
                for j in range(chunks):
                    part[j, :, at + lo : at + hi] = r[j * W : (j + 1) * W]
                here = jnp.max(jnp.abs(r), axis=0, keepdims=True)
                if hi - lo < 256:
                    largest.append(jnp.max(here, axis=1, keepdims=True))
                else:
                    peak = jnp.maximum(peak, here)
            largest.append(jnp.max(peak, axis=1, keepdims=True))
        top_g, top_a = jnp.maximum(largest[0], largest[1]), jnp.maximum(largest[2], largest[3])
        for j in range(chunks):
            part[j, :, nf:base] = jnp.zeros((W, base - nf), F32)
            part[j, :, base + na :] = jnp.zeros((W, lanes - base - na), F32)
        lane = lax.broadcasted_iota(jnp.int32, (8, 128), 1)
        hy[0] = jnp.maximum(jnp.where(lane < 64, top_g, top_a), 1e-30)
        state["first"] = [TOP / b for b in bounds(hy[0])]
        pl.semaphore_wait(barrier, len(partners))
        fan(hny, [(hy.at[0], hy.at[i], yz(i, 0)) for i in range(1, NY)], group(hy.at[1:NY]))

    def scale_y():
        landed(hny, hy.at[1:NY])
        hz[0] = hy[0] + hy[1] + hy[2] + hy[3]
        for i in (1, 3):
            state["y", i] = [b * (1.0 / TOP) for b in bounds(hy[i])]
        fan(hnz, [(hz.at[0], hz.at[i], yz(0, i)) for i in range(1, NZ)], group(hz.at[1:NZ]))
        state["unit"] = [b * (1.0 / TOP) for b in bounds(hz[0])]
        state["scale"] = [TOP / b for b in bounds(hz[0])]

    def scale_z():
        landed(hnz, hz.at[1:NZ])
        for turn in (1, -1):
            for mine, over in ((0, turn), (0, -turn)):
                total = hz[0] + hz[over % NZ]
                state["two", over % NZ] = [TOP / b for b in bounds(total)]
            for k in (1, 3, -2):
                total = hz[turn * k % NZ] + hz[turn * (k + (1 if k > 0 else -1)) % NZ]
                state["sum", turn * k % NZ] = [b * (1.0 / TOP) for b in bounds(total)]
            state["z", turn % NZ] = [b * (1.0 / TOP) for b in bounds(hz[turn % NZ])]

    begin = plan.task(rot, 4.0, sends=[(hny, "y0", 0.0)])
    scaled = plan.task(scale_y, 0.3, after=[begin], arrivals=[hny], sends=[(hnz, "zz", 0.0)], rank=-1)
    begin2 = plan.task(scale_z, 0.3, after=[scaled], arrivals=[hnz], rank=-1)
    chain = {"t0": [begin], "t1": [], "t2": []}

    ready = []
    for j in range(chunks):
        rank = j
        size = rows * wide * 2e-3
        signs = (1, -1)
        n = [[plan.message() for _ in range(3)] for _ in signs]
        gy, gz, gz2, gy2 = group(ysend.at[j]), group(zbuf.at[j, 1:NZ]), group(zbuf.at[j, 1:NZ]), group(ysend.at[j])
        turn = 1 if j % 2 == 0 else -1

        def rs0(j=j, n=n, gy=gy):
            for h, sg in enumerate(signs):
                d = wrap(y + 2 * sg, NY)
                ysend[j, h, 0] = encode(piece(j, h, d)[...], spread(state["first"], d))
                post(n[h][0], ysend.at[j, h, 0], ybuf.at[j, h, 0], yz(sg, 0), gy)

        def rs1(j=j, n=n, gy=gy):
            for h, sg in enumerate(signs):
                d = wrap(y - sg, NY)
                ysend[j, h, 2] = encode(piece(j, h, d)[...], spread(state["first"], d))
                post(n[h][2], ysend.at[j, h, 2], ybuf.at[j, h, 2], yz(-sg, 0), gy)

        def rs2(h, sg, j=j, n=n, gy=gy):
            d = wrap(y + sg, NY)
            landed(n[h][0], ybuf.at[j, h, 0])
            total = piece(j, h, d)[...] + decode(ybuf[j, h, 0], spread(state["y", sg % NY], d))
            ysend[j, h, 1] = encode(total, spread(state["scale"], d))
            post(n[h][1], ysend.at[j, h, 1], ybuf.at[j, h, 1], yz(sg, 0), gy)

        zn = [plan.message() for _ in range(4)]

        def zrows(ref, step, j=j):
            return block(ref.at[j], wrap(z + step, NZ) * short, short, 0, wide)

        def middle(j=j, n=n, zn=zn, gz=gz, t=turn, zrows=zrows):
            unit, scale = spread(state["unit"], y), spread(state["scale"], y)
            other = [spread(state["y", -sg % NY], y) for sg in signs]
            for h in (0, 1):
                landed(n[h][1], ybuf.at[j, h, 1])
                landed(n[h][2], ybuf.at[j, h, 2])
                total = piece(j, h, y)[...] + decode(ybuf[j, h, 1], unit) + decode(ybuf[j, h, 2], other[h])
                acc[j, h * rows : (h + 1) * rows, :] = total
                zsend[j, h * rows : (h + 1) * rows, :] = encode(total, scale)
            fan(zn[0], [(zrows(zsend, 4), zbuf.at[j, 0], yz(0, t)), (zrows(zsend, 2 * t), zbuf.at[j, 1], yz(0, t)),
                        (zrows(zsend, -3 * t), zbuf.at[j, 2], yz(0, -t))], gz)
            fan(zn[1], [(zrows(zsend, -t), zbuf.at[j, 3], yz(0, -t))], gz)

        def relay_z(j=j, zn=zn, gz=gz, t=turn, zrows=zrows):
            landed(zn[0], zbuf.at[j, 0:3])
            near = spread(state["z", t % NZ], y)
            far = spread(state["z", -t % NZ], y)
            ahead, back = spread(state["two", t % NZ], y), spread(state["two", -t % NZ], y)
            for k, (got, step, unit, scale) in enumerate(((0, 3 * t, near, ahead), (1, t, near, ahead), (2, -2 * t, far, back))):
                relayed[j, k] = encode(zrows(acc, step)[...] + decode(zbuf[j, got], unit), scale)
            fan(zn[1], [(relayed.at[j, k], zbuf.at[j, 4 + k], yz(0, step)) for k, step in ((0, 3 * t), (1, t), (2, -2 * t))], gz)

        def finish(j=j, zn=zn, gz2=gz2, t=turn, zrows=zrows):
            landed(zn[1], zbuf.at[j, 3:7])
            total = zrows(acc, 0)[...] + decode(zbuf[j, 3], spread(state["z", -t % NZ], y))
            for k, step in ((4, 3 * t), (5, t), (6, -2 * t)):
                total = total + decode(zbuf[j, k], spread(state["sum", step % NZ], y))
            mine = block(fin.at[j], z * short, short, y * wide, wide)
            mine[...] = total.astype(BF16)
            fan(zn[2], [(mine, mine, yz(0, step)) for step in (3 * t, t, -t, -2 * t)], gz2)

        def spread_z(j=j, zn=zn, gz2=gz2, t=turn):
            landed(zn[2], zbuf.at[j, 0:4])
            for step, to in ((-3 * t, t), (-t, t), (2 * t, -t)):
                got = block(fin.at[j], wrap(z + step, NZ) * short, short, y * wide, wide)
                fan(zn[3], [(got, got, yz(0, to))], gz2)

        a = [plan.message() for _ in range(6)]

        def fin_half(j, h, d):
            return block(fin.at[j], h * rows, rows, d * wide, wide)

        def ag0(zn=zn, a=a, j=j, gy2=gy2):
            landed(zn[3], zbuf.at[j, 0:3])
            for h, sg in enumerate(signs):
                mine = fin_half(j, h, y)
                post(a[3 * h], mine, mine, yz(sg, 0), gy2)
            for h, sg in enumerate(signs):
                mine = fin_half(j, h, y)
                post(a[3 * h + 2], mine, mine, yz(-sg, 0), gy2)

        def ag1(h, sg, a=a, j=j, gy2=gy2):
            got = fin_half(j, h, wrap(y - sg, NY))
            landed(a[3 * h], got)
            post(a[3 * h + 1], got, got, yz(sg, 0), gy2)

        def complete(a=a, j=j):
            for h, sg in enumerate(signs):
                landed(a[3 * h + 1], fin_half(j, h, wrap(y - 2 * sg, NY)))
                landed(a[3 * h + 2], fin_half(j, h, wrap(y + sg, NY)))
            if j == 0:
                for one in local[4:]:
                    one.wait()

        t0 = plan.task(rs0, 0.3, after=chain["t0"], sends=[(n[0][0], "y1", size), (n[1][0], "y-1", size)], rank=rank)
        t1 = plan.task(rs1, 0.3, after=chain["t1"] + [t0], sends=[(n[0][2], "y-1", size), (n[1][2], "y1", size)], rank=rank)
        t2 = []
        for h, sg in enumerate(signs):
            def rs2_of(h=h, sg=sg, rs2=rs2):
                rs2(h, sg)

            rs2_of.__name__ = "rs2"
            t2.append(plan.task(rs2_of, 0.3, after=[t0, scaled], arrivals=[n[h][0]], sends=[(n[h][1], "y%d" % sg, size)], rank=rank))
        chain["t0"], chain["t1"] = [t1] if j == 0 else chain["t2"], t2
        chain["t2"] = t2
        unit_z = short * wide * 2e-3
        t3 = plan.task(middle, 0.6, after=t2 + [t1], arrivals=[n[0][1], n[0][2], n[1][1], n[1][2]],
                       sends=[(zn[0], "z%d" % turn, 2 * unit_z), (zn[1], "z%d" % -turn, 2 * unit_z)], rank=rank)
        t3 = plan.task(relay_z, 0.3, after=[t3, begin2], arrivals=[zn[0]],
                       sends=[(zn[1], "z%d" % turn, 4 * unit_z), (n[0][0], "z%d" % -turn, 2 * unit_z)], rank=rank)
        t4 = plan.task(finish, 0.3, after=[t3], arrivals=[zn[1]],
                       sends=[(zn[2], "z%d" % turn, 4 * unit_z), (n[0][0], "z%d" % -turn, 3 * unit_z)], rank=rank)
        t4 = plan.task(spread_z, 0.1, after=[t4], arrivals=[zn[2]],
                       sends=[(zn[3], "z%d" % turn, 2 * unit_z), (n[0][0], "z%d" % -turn, unit_z)], rank=rank)
        t5 = plan.task(ag0, 0.2, after=[t4], arrivals=[zn[3]], sends=[(a[0], "y1", size), (a[3], "y-1", size), (a[2], "y-1", size), (a[5], "y1", size)], rank=rank)
        t6 = []
        for h, sg in enumerate(signs):
            def ag1_of(h=h, sg=sg, ag1=ag1):
                ag1(h, sg)

            ag1_of.__name__ = "ag1"
            t6.append(plan.task(ag1_of, 0.1, after=[t5], arrivals=[a[3 * h]], sends=[(a[3 * h + 1], "y%d" % sg, size)], rank=rank))
        ready.append(plan.task(complete, 0.1, after=t6, arrivals=[a[1], a[2], a[4], a[5]], rank=rank))

    size4 = 4 * tile * own * 4e-3
    size2 = each * (count + 128) * 2e-3
    pairs[...] = jnp.zeros(pairs.shape, F32)
    log2 = 1.0 / math.log(2.0)

    def pack(dst, value):
        bound = jnp.maximum(jnp.max(jnp.max(jnp.abs(value), axis=0, keepdims=True), axis=1, keepdims=True), 1e-30)
        power = jnp.ceil(jnp.log(bound) * log2)
        dst[:, :count] = encode(value, TOP * jnp.exp(power * (-1.0 / log2)))
        dst[:, count:] = jnp.broadcast_to(power, (each, 128)).astype(jnp.int32).astype(I16)

    def unpack(src):
        power = src[:, count:].astype(jnp.int32).astype(F32)[0:1, 0:1]
        return decode(src[:, :count], jnp.exp(power * (1.0 / log2)) * (1.0 / TOP))

    for j in range(chunks):
        rank = 10 + j
        to_core = plan.message()
        gc, gx = group(precv.at[j]), group(xs.at[j])

        def theirs_block(j, i):
            return pfull.at[j, :, pl.ds(pl.multiple_of((1 - c) * own, 16), own), 2 * i * tile : 2 * (i + 1) * tile]

        def there_block(j, i):
            return precv.at[j, :, :, 2 * i * tile : 2 * (i + 1) * tile]

        prev = [ready[j]]
        for i in range(8):
            def project(i=i, j=j, gc=gc, to_core=to_core, theirs_block=theirs_block, there_block=there_block):
                token = slice(i * tile, (i + 1) * tile)
                pfull[j, 0, :, token] = jnp.dot(fin[j, :, :nf], xg[:, token], preferred_element_type=F32)
                pfull[j, 1, :, token] = lax.dot_general(
                    fin[j, :, base : base + na], xa[token, :], (((1,), (1,)), ((), ())), preferred_element_type=F32)
                if i % 2:
                    post(to_core, theirs_block(j, i // 2), there_block(j, i // 2), across(0, 1), gc)

            prev = [plan.task(project, 0.27, after=prev, sends=[(to_core, "core", size4)] if i % 2 else [], rank=rank)]
        m = [plan.message() for _ in range(6)]

        def pair(k, dx, j=j):
            to = wrap(x + dx, NX) * each
            return (pfull[j, k, pl.ds(pl.multiple_of(c * own + to, 16), each), :]
                    + precv[j, k, pl.ds(pl.multiple_of(to, 16), each), :])

        def send(k, value, dx, j=j, m=m, gx=gx):
            pack(xs.at[j, k], value)
            post(m[k], xs.at[j, k], xr.at[j, k], across(dx), gx)

        def arrived(k, j=j, m=m):
            landed(m[k], xr.at[j, k])
            return unpack(xr.at[j, k])

        def far(j=j, send=send, pair=pair, to_core=to_core):
            landed(to_core, precv.at[j])
            send(0, pair(0, 2), 1)
            send(1, pair(1, 2), -1)

        def near(send=send, pair=pair):
            send(2, pair(0, -1), -1)
            send(3, pair(1, 1), 1)

        def relay(send=send, arrived=arrived, pair=pair):
            send(4, pair(0, 1) + arrived(0), 1)
            send(5, pair(1, -1) + arrived(1), -1)

        def score(arrived=arrived, pair=pair):
            g = pair(0, 0) + arrived(2) + arrived(4)
            a = pair(1, 0) + arrived(3) + arrived(5)
            pairs[...] += g * a

        a1 = plan.task(far, 0.5, after=prev, arrivals=[to_core],
                       sends=[(m[0], "x1", size2), (m[1], "x-1", size2)], rank=rank)
        a2 = plan.task(near, 0.4, after=[a1], sends=[(m[2], "x-1", size2), (m[3], "x1", size2)], rank=rank)
        a3 = plan.task(relay, 0.6, after=[a2], arrivals=[m[0], m[1]], sends=[(m[4], "x1", size2), (m[5], "x-1", size2)], rank=rank)
        plan.task(score, 0.6, after=[a3], arrivals=[m[2], m[3], m[4], m[5]], rank=rank)

    for at in plan.order():
        plan.tasks[at][0]()

    used = plan.messages
    token = lax.broadcasted_iota(jnp.int32, (2, count), 1)
    first, both = lens[0], lens[0] + lens[1]
    summed = jnp.sum(pairs[...].reshape(2, each // 2, count), axis=1)
    by_example = [jnp.sum(jnp.where(mask, summed, 0.0), axis=1, keepdims=True)
                  for mask in (token < first, (token >= first) & (token < both))]
    factor = 1.0 / math.sqrt(LMAX * RANK)
    row = lax.broadcasted_iota(jnp.int32, (8, 128), 0)
    lane = lax.broadcasted_iota(jnp.int32, (8, 128), 1)
    score_of = jnp.where(row == 0, jnp.where(lane == 0, by_example[0][0:1], by_example[0][1:2]),
                         jnp.where(lane == 0, by_example[1][0:1], by_example[1][1:2]))
    named = jnp.where(row == 0, dest[0], jnp.where(row == 1, dest[1], -1)).astype(F32)
    exbuf[0] = jnp.where(lane == 2, named, score_of * factor)
    hops = lambda i: min(i // NZ, NY - i // NZ) + min(i % NZ, NZ - i % NZ)
    order = sorted(range(1, NY * NZ), key=lambda i: (-hops(i), i))
    fan(used, [(exbuf.at[0], exbuf.at[i], yz(i // NZ, i % NZ)) for i in order], group(exbuf.at[1 : NY * NZ]))
    landed(used, exbuf.at[1 : NY * NZ])
    every = exbuf[...].reshape(NY * NZ * 8, 128)
    target = every[:, 2:3]
    picked = [jnp.sum(jnp.where(target == (2 * ex + r).astype(F32), every, 0.0), axis=0, keepdims=True)[:, 0:2] for r in range(2)]
    out[...] = jnp.where(lax.broadcasted_iota(jnp.int32, (2, 2), 0) == 0, picked[0], picked[1])

    for one in sent:
        one.wait_send()


def shards(acts, grads, act_basis, grad_basis, act_query, grad_query, lengths, destination):
    grads, act_basis, grad_basis = grads.T, act_basis.T, grad_basis.T
    count, na = acts.shape
    nf = grads.shape[0]
    columns = grad_query.shape[1]
    chunks = columns // W
    tiles = -(-nf // 128) + -(-na // 128)
    lanes = -(-tiles // NY) * NY * 128
    short, wide = W // NZ, lanes // NY
    any_ = pl.BlockSpec(memory_space=pl.ANY)
    smem = pl.BlockSpec(memory_space=pltpu.SMEM)
    messages, groups = 2 + chunks * 23 + 2, 4 + chunks * 6
    return pl.pallas_call(
        kernel,
        out_shape=jax.ShapeDtypeStruct((2, 2), F32),
        in_specs=[smem, smem] + [any_] * 6,
        out_specs=pl.BlockSpec(memory_space=pltpu.VMEM),
        scratch_shapes=[
            pltpu.VMEM(acts.shape, BF16),
            pltpu.VMEM(grads.shape, BF16),
            pltpu.VMEM(act_basis.shape, BF16),
            pltpu.VMEM(grad_basis.shape, BF16),
            pltpu.VMEM(act_query.shape, BF16),
            pltpu.VMEM(grad_query.shape, BF16),
            pltpu.VMEM(act_query.shape[::-1], BF16),
            pltpu.VMEM(grad_query.shape[::-1], BF16),
            pltpu.VMEM((chunks, W, lanes), F32),
            pltpu.VMEM((chunks, W, lanes), BF16),
            pltpu.VMEM((chunks, 2, 3, W // 2, wide), I16),
            pltpu.VMEM((chunks, 2, 3, W // 2, wide), I16),
            pltpu.VMEM((chunks, W, wide), F32),
            pltpu.VMEM((chunks, W, wide), I16),
            pltpu.VMEM((chunks, NZ, short, wide), I16),
            pltpu.VMEM((chunks, 3, short, wide), I16),
            pltpu.VMEM((NY, 8, 128), F32),
            pltpu.VMEM((NZ, 8, 128), F32),
            pltpu.VMEM((chunks, 2, W, count), F32),
            pltpu.VMEM((chunks, 2, W // 2, count), F32),
            pltpu.VMEM((chunks, 6, W // (2 * NX), count + 128), I16),
            pltpu.VMEM((chunks, 6, W // (2 * NX), count + 128), I16),
            pltpu.VMEM((W // (2 * NX), count), F32),
            pltpu.VMEM((NY * NZ, 8, 128), F32),
            pltpu.SemaphoreType.DMA((6,)),
            pltpu.SemaphoreType.DMA((groups,)),
            pltpu.SemaphoreType.DMA((messages,)),
        ],
        compiler_params=pltpu.CompilerParams(collective_id=0, has_side_effects=True, vmem_limit_bytes=60 << 20),
        name="influence",
    )(lengths, destination, acts, grads, act_basis, grad_basis, act_query, grad_query)


def solution(mesh):
    return jax.shard_map(
        shards,
        mesh=mesh,
        in_specs=(
            P("ex", "lay"),
            P("ex", "lay"),
            P("lay", "ex"),
            P("lay", "ex"),
            P("ex", None),
            P("ex", None),
            P("ex"),
            P("ex"),
        ),
        out_specs=P("ex", "lay"),
        check_vma=False,
    )
```

time: 111 us -> 89.2 us (0.80)
  Pallas kernels: 108 us -> 87.2 us
    pallas_call x1, Pallas kernels: 108 us -> 87.2 us  [shards(): pl.pallas_call(kernel, out_shape=jax.ShapeDtypeStruct((2, 2), F32), in_sp...]
where the time goes in v3:
time: 89.2 us; the launch traced here: 88.4 us
  Pallas kernels  87.2 us (98%)
  local copies, waits for them, and re-layouts  1.24 us (1%)
    pallas_call x1, Pallas kernels, shards(): pl.pallas_call(kernel, out_shape=jax.ShapeDtypeStruct((2, 2), F32), in_sp...  87.2 us

profile of v3, /device:TPU:8, one launch (start us, length us, event | category | flops | bytes accessed | tf_op | source)
XLA Modules:
  0.0 88.4 jit_solution(3959628950939332262)
XLA Ops:
  0.0 87.2 %influence.1 = f32[2,2]{1,0:T(2,128)} custom-call(s32[2]{0:T(128)} %lens.1, s32[2]{0:T(128)} %dest.1, bf16[2048,640]{1,0:T(8,128)(2,1)} %acts.1, bf16[1728,2048]{1,0:T(8,128)(2,1)} %bitcast.3, bf16[160,640]{1,0:T(8,128)(2,1)} %bitcast.5, bf16[432,1728]{1,0:T(8,128)(2,1)} %bitcast.4, bf16[160,512]{1,0:T(8,128)(2,1)} %aquery.1, bf16[432,512]{1,0:T(8,128)(2,1)} %gquery.1), custom_call_target="tpu_custom_call" | custom-call | tf_op jit(solution)/shard_map/influence/pallas_call | solution.py:460
  87.2 1.2 %copy.10 = f32[2,2]{1,0:T(2,128)} copy(f32[2,2]{1,0:T(2,128)} %influence.1) | data formatting | bytes 32

commit v4 on v3

--- a/solution.py
+++ b/solution.py
@@ -35,8 +35,33 @@
         self.tasks.append((emit, cost, tuple(after), tuple(arrivals), tuple(sends), rank))
         return len(self.tasks) - 1
 
+    def levels(self):
+        level = [0.0] * len(self.tasks)
+        users = [[] for _ in self.tasks]
+        waits = {}
+        for at, (_, _, after, arrivals, _, _) in enumerate(self.tasks):
+            for a in after:
+                users[a].append(at)
+            for m in arrivals:
+                waits.setdefault(m, []).append(at)
+        for _ in range(len(self.tasks)):
+            changed = False
+            for at in reversed(range(len(self.tasks))):
+                _, cost, _, _, sends, _ = self.tasks[at]
+                best = max([level[u] for u in users[at]], default=0.0)
+                for number, link, size in sends:
+                    flight = 2.2 + size / 0.05 * 1e-3 if link != "core" else 1.0 + size / 0.3 * 1e-3
+                    best = max([best] + [flight + level[u] for u in waits.get(number, [])])
+                if cost + best > level[at] + 1e-9:
+                    level[at] = cost + best
+                    changed = True
+            if not changed:
+                break
+        return level
+
     def order(self):
         now, done, arrived, link_free, left, out = 0.0, {}, {}, {}, list(range(len(self.tasks))), []
+        level = self.levels()
         while left:
             best = None
             for at in left:
@@ -44,7 +69,7 @@
                 if any(a not in done for a in after) or any(m not in arrived for m in arrivals):
                     continue
                 start = max([now] + [arrived[m] for m in arrivals])
-                key = (start, rank, at)
+                key = (start, -level[at], at)
                 if best is None or key < best:
                     best = key
             start, _, at = best
@@ -52,7 +77,7 @@
             now = start + cost
             done[at] = now
             for number, link, size in sends:
-                rate, latency = (0.3, 2.5) if link == "core" else (0.062, 4.0 if link[0] == "x" else 2.2)
+                rate, latency = (0.3, 2.5) if link == "core" else (0.045, 4.0 if link[0] == "x" else 2.2)
                 begin = max(now, link_free.get(link, 0.0))
                 link_free[link] = begin + size / rate * 1e-3
                 arrived[number] = link_free[link] + latency
@@ -361,10 +386,10 @@
         gc, gx = group(precv.at[j]), group(xs.at[j])
 
         def theirs_block(j, i):
-            return pfull.at[j, :, pl.ds(pl.multiple_of((1 - c) * own, 16), own), 2 * i * tile : 2 * (i + 1) * tile]
+            return pfull.at[j, :, pl.ds(pl.multiple_of((1 - c) * own, 16), own), 4 * i * tile : 4 * (i + 1) * tile]
 
         def there_block(j, i):
-            return precv.at[j, :, :, 2 * i * tile : 2 * (i + 1) * tile]
+            return precv.at[j, :, :, 4 * i * tile : 4 * (i + 1) * tile]
 
         prev = [ready[j]]
         for i in range(8):
@@ -373,10 +398,10 @@
                 pfull[j, 0, :, token] = jnp.dot(fin[j, :, :nf], xg[:, token], preferred_element_type=F32)
                 pfull[j, 1, :, token] = lax.dot_general(
                     fin[j, :, base : base + na], xa[token, :], (((1,), (1,)), ((), ())), preferred_element_type=F32)
-                if i % 2:
-                    post(to_core, theirs_block(j, i // 2), there_block(j, i // 2), across(0, 1), gc)
-
-            prev = [plan.task(project, 0.27, after=prev, sends=[(to_core, "core", size4)] if i % 2 else [], rank=rank)]
+                if i % 4 == 3:
+                    post(to_core, theirs_block(j, i // 4), there_block(j, i // 4), across(0, 1), gc)
+
+            prev = [plan.task(project, 0.27, after=prev, sends=[(to_core, "core", 2 * size4)] if i % 4 == 3 else [], rank=rank)]
         m = [plan.message() for _ in range(6)]
 
         def pair(k, dx, j=j):

time: 89.2 us -> 86.6 us (0.971)
  Pallas kernels: 87.2 us -> 85 us
    pallas_call x1, Pallas kernels: 87.2 us -> 85 us  [shards(): pl.pallas_call(kernel, out_shape=jax.ShapeDtypeStruct((2, 2), F32), in_sp...]
where the time goes in v4:
time: 86.6 us; the launch traced here: 86.3 us
  Pallas kernels  85 us (98%)
  local copies, waits for them, and re-layouts  1.24 us (1%)
    pallas_call x1, Pallas kernels, shards(): pl.pallas_call(kernel, out_shape=jax.ShapeDtypeStruct((2, 2), F32), in_sp...  85 us

profile of v4, /device:TPU:8, one launch (start us, length us, event | category | flops | bytes accessed | tf_op | source)
XLA Modules:
  0.0 86.3 jit_solution(3699695319222337282)
XLA Ops:
  0.0 85.0 %influence.1 = f32[2,2]{1,0:T(2,128)} custom-call(s32[2]{0:T(128)} %lens.1, s32[2]{0:T(128)} %dest.1, bf16[2048,640]{1,0:T(8,128)(2,1)} %acts.1, bf16[1728,2048]{1,0:T(8,128)(2,1)} %bitcast.3, bf16[160,640]{1,0:T(8,128)(2,1)} %bitcast.5, bf16[432,1728]{1,0:T(8,128)(2,1)} %bitcast.4, bf16[160,512]{1,0:T(8,128)(2,1)} %aquery.1, bf16[432,512]{1,0:T(8,128)(2,1)} %gquery.1), custom_call_target="tpu_custom_call" | custom-call | tf_op jit(solution)/shard_map/influence/pallas_call | solution.py:485
  85.0 1.2 %copy.10 = f32[2,2]{1,0:T(2,128)} copy(f32[2,2]{1,0:T(2,128)} %influence.1) | data formatting | bytes 32
